TPU v7x, 32 devices: a whole 2x2x4 slice. The times are simulated.
32 devices in a mesh: dp: 8 (over y, x, core), tensor: 4 (over z).
Axes of the slice: x: 2, y: 2, z: 4, core: 2. Of those that a mesh axis runs over, the one named last changes fastest.
Arguments:
- queries: bfloat16 [1024, 16384], P('dp', 'tensor'), may hold values from -24 to 24
- draft_keys: bfloat16 [1024, 1024], P('dp'), may hold values from -6 to 6
- draft_values: bfloat16 [1024, 1024], P('dp'), may hold values from -6 to 6
- cache_keys: bfloat16 [16, 2048, 1024], P('dp', 'tensor'), may hold values from -24 to 24
- cache_values: bfloat16 [16, 2048, 1024], P('dp', 'tensor'), may hold values from -6 to 6
- out_weight: bfloat16 [16384, 16384], P('tensor', 'dp'), may hold values from -0.25 to 0.25
- cache_lengths: int32 [16], P('dp'), may hold values from 512 to 2048
- draft_lengths: int32 [16], replicated, may hold values from 8 to 64
- dest_group: int32 [16], replicated, may hold values from 0 to 7, as said below
- dest_offset: int32 [16], replicated, may hold values from 0 to 32, as said below
Outputs:
- verified: bfloat16 [768, 16384], P('tensor', 'dp')
Inputs may be any that keep to these rules, and one draw needn't show every extreme that they name: `dest_group`: at most one request of a group has another group as destination, and each group receives at most one such request. `dest_offset`: blocks with the same destination never intersect and end at packed row 96 or before; a block moved to another group starts right after that group's own rows; in every draw some group's blocks fill all 96 rows.
All inputs are finite; a program needn't handle non-finite values.
Results may differ from a plain program's by a relative error of at most 0.017.
Values may be sent and summed in bfloat16 or wider, within the bound.
A program may use at most 128 MiB of HBM per device.

v0:
```python
import jax
import jax.numpy as jnp
from jax import lax
from jax.sharding import PartitionSpec as P

HEADS = 128
KV_HEADS = 8
HEAD_DIM = 128
DRAFT = 64
GROUP_REQ = 2
CACHE = 2048
PACK = 96


NEG_FILL = -1e30


def packed_sources(row_ids, draft_lengths, dest_group, dest_offset):
    request_ids = jnp.arange(dest_group.shape[0], dtype=jnp.int32)
    slot_group = row_ids // PACK
    slot_index = row_ids % PACK
    inside = (
        (dest_group[None, :] == slot_group[:, None])
        & (slot_index[:, None] >= dest_offset[None, :])
        & (slot_index[:, None] < (dest_offset + draft_lengths)[None, :])
    )
    request = jnp.sum(jnp.where(inside, request_ids[None, :], 0), axis=1)
    first_slot = jnp.sum(jnp.where(inside, dest_offset[None, :], 0), axis=1)
    return (request, slot_index - first_slot, jnp.any(inside, axis=1))


def attend_one(operands):
    queries_one, cache_k, cache_v, draft_k, draft_v, cache_len, draft_len = operands
    score_scale = HEAD_DIM ** (-0.5)
    cache_scores = (
        jnp.einsum("qkgd,lkd->kgql", queries_one, cache_k, preferred_element_type=jnp.float32)
        * score_scale
    )
    draft_scores = (
        jnp.einsum("qkgd,jkd->kgqj", queries_one, draft_k, preferred_element_type=jnp.float32)
        * score_scale
    )
    cache_pos = jnp.arange(cache_k.shape[0], dtype=jnp.int32)
    draft_pos = jnp.arange(draft_k.shape[0], dtype=jnp.int32)
    keep_cache = cache_pos < cache_len
    keep_draft = (draft_pos[None, :] <= draft_pos[:, None]) & (draft_pos[None, :] < draft_len)
    cache_scores = jnp.where(keep_cache, cache_scores, NEG_FILL)
    draft_scores = jnp.where(keep_draft, draft_scores, NEG_FILL)
    highest = jnp.maximum(
        jnp.max(cache_scores, axis=-1, keepdims=True), jnp.max(draft_scores, axis=-1, keepdims=True)
    )
    cache_exp = jnp.exp(cache_scores - highest)
    draft_exp = jnp.exp(draft_scores - highest)
    denominator = jnp.sum(cache_exp, axis=-1, keepdims=True) + jnp.sum(
        draft_exp, axis=-1, keepdims=True
    )
    cache_weights = (cache_exp / denominator).astype(jnp.bfloat16)
    draft_weights = (draft_exp / denominator).astype(jnp.bfloat16)
    mixed = jnp.einsum("kgql,lkd->qkgd", cache_weights, cache_v, preferred_element_type=jnp.float32)
    mixed = mixed + jnp.einsum(
        "kgqj,jkd->qkgd", draft_weights, draft_v, preferred_element_type=jnp.float32
    )
    is_live = draft_pos < draft_len
    return jnp.where(is_live[:, None, None, None], mixed, 0.0).astype(jnp.bfloat16)


def body(
    queries,
    draft_keys,
    draft_values,
    cache_keys,
    cache_values,
    out_weight,
    cache_lengths,
    draft_lengths,
    dest_group,
    dest_offset,
):
    tensor_count = lax.axis_size("tensor")
    data_count = lax.axis_size("dp")
    my_rank = lax.axis_index("tensor")
    my_group = lax.axis_index("dp")
    local_heads = HEADS // tensor_count
    group_heads = HEADS // KV_HEADS
    kv_local = max(1, local_heads // group_heads)
    per_kv = local_heads // kv_local
    kv_width = kv_local * HEAD_DIM
    span_rows = cache_keys.shape[1]
    if tensor_count >= KV_HEADS:
        copies = tensor_count // KV_HEADS

        def spread(cache_block):
            return jnp.repeat(
                cache_block.reshape(GROUP_REQ, span_rows, KV_HEADS, HEAD_DIM), copies, axis=2
            )

    else:

        def spread(cache_block):
            return cache_block.reshape(GROUP_REQ, span_rows, tensor_count, kv_width)

    full_keys, full_values = (
        lax.all_to_all(spread(cache_keys), "tensor", split_axis=2, concat_axis=1, tiled=True),
        lax.all_to_all(spread(cache_values), "tensor", split_axis=2, concat_axis=1, tiled=True),
    )
    full_keys = full_keys.reshape(GROUP_REQ, CACHE, kv_local, HEAD_DIM)
    full_values = full_values.reshape(GROUP_REQ, CACHE, kv_local, HEAD_DIM)
    kv_first = my_rank * local_heads // group_heads
    draft_k = lax.dynamic_slice_in_dim(draft_keys, kv_first * HEAD_DIM, kv_width, 1).reshape(
        GROUP_REQ, DRAFT, kv_local, HEAD_DIM
    )
    draft_v = lax.dynamic_slice_in_dim(draft_values, kv_first * HEAD_DIM, kv_width, 1).reshape(
        GROUP_REQ, DRAFT, kv_local, HEAD_DIM
    )
    local_queries = queries.reshape(GROUP_REQ, DRAFT, kv_local, per_kv, HEAD_DIM)
    my_lengths = lax.dynamic_slice_in_dim(draft_lengths, my_group * GROUP_REQ, GROUP_REQ)
    attended = lax.map(
        attend_one,
        (local_queries, full_keys, full_values, draft_k, draft_v, cache_lengths, my_lengths),
    )
    width_local = local_heads * HEAD_DIM
    attended_rows = attended.reshape(GROUP_REQ * DRAFT, width_local)
    target_rows = PACK * data_count // tensor_count
    home_all = lax.all_gather(attended_rows, "dp", axis=0, tiled=True)
    row_ids = jnp.arange(lax.axis_size("tensor") * target_rows, dtype=jnp.int32)
    request, within, is_live = packed_sources(row_ids, draft_lengths, dest_group, dest_offset)
    picked = jnp.take(home_all, request * DRAFT + within, axis=0)
    picked = jnp.where(is_live[:, None], picked, jnp.zeros((), jnp.bfloat16))
    return lax.psum_scatter(
        jnp.dot(picked, out_weight, preferred_element_type=jnp.float32).astype(jnp.bfloat16),
        "tensor",
        scatter_dimension=0,
        tiled=True,
    )


def solution(mesh):
    in_specs = (
        P("dp", "tensor"),
        P("dp", None),
        P("dp", None),
        P("dp", "tensor", None),
        P("dp", "tensor", None),
        P("tensor", "dp"),
        P("dp"),
        P(),
        P(),
        P(),
    )
    out_specs = P("tensor", "dp")
    return jax.shard_map(body, mesh=mesh, in_specs=in_specs, out_specs=out_specs, check_vma=False)
```

profile of v0, /device:TPU:10, one launch (start us, length us, event | category | flops | bytes accessed | tf_op | source)
XLA Modules:
  0.0 319.0 jit_solution(13467972489763568803)
XLA Ops:
  6.5 2.9 copy.45
  9.4 2.4 copy.46
  11.8 5.3 %all-to-all-start = ((bf16[2,512,4,256]{3,1,0,2:T(8,128)(2,1)}), bf16[2,512,4,256]{3,1,0,2:T(8,128)(2,1)S(1)}, u32[]{:S(2)}, u32[]{:S(2)}) async-start(bf16[2,512,4,256]{3,1,0,2:T(8,128)(2,1)} %copy.46), calls=%async_computation | async-start | bytes 4194304 | tf_op jit(solution)/shard_map/all_to_all | solution.py:104
  17.1 0.0 copy-start.3
  17.1 4.0 %copy.48 = bf16[2,512,1024]{1,2,0:T(8,128)(2,1)} copy(bf16[2,512,1024]{2,1,0:T(8,128)(2,1)} %param.15) | data formatting | bytes 4194304 | tf_op args[3]
  21.1 4.1 %copy.49 = bf16[2,512,4,256]{3,1,0,2:T(8,128)(2,1)} copy(bf16[2,512,4,256]{1,3,2,0:T(8,128)(2,1)} %bitcast.105) | data formatting | bytes 4194304 | tf_op jit(solution)/shard_map/reshape | solution.py:100
  25.2 36.8 %all-to-all-done = bf16[2,512,4,256]{3,1,0,2:T(8,128)(2,1)S(1)} async-done(((bf16[2,512,4,256]{3,1,0,2:T(8,128)(2,1)}), bf16[2,512,4,256]{3,1,0,2:T(8,128)(2,1)S(1)}, u32[]{:S(2)}, u32[]{:S(2)}) %all-to-all-start) | async-done | bytes 2097184 | tf_op jit(solution)/shard_map/all_to_all | solution.py:104
  62.0 7.7 %all-to-all-start.1 = ((bf16[2,512,4,256]{3,1,0,2:T(8,128)(2,1)}), bf16[2,512,4,256]{3,1,0,2:T(8,128)(2,1)}, u32[]{:S(2)}, u32[]{:S(2)}) async-start(bf16[2,512,4,256]{3,1,0,2:T(8,128)(2,1)} %copy.49), calls=%async_computation.1 | async-start | bytes 4194304 | tf_op jit(solution)/shard_map/all_to_all | solution.py:103
  69.7 0.0 all-gather.2.cloned.1.call-start
  69.7 0.9 constant_dynamic-slice_fusion.5
  70.6 1.4 copy.69
  72.1 0.0 copy-done.3
  72.1 0.1 dynamic_slice.34
  72.2 0.0 copy-start.2
  72.2 1.5 copy.47
  73.7 2.5 reshape.121
  76.2 37.9 %all-to-all-done.1 = bf16[2,512,4,256]{3,1,0,2:T(8,128)(2,1)} async-done(((bf16[2,512,4,256]{3,1,0,2:T(8,128)(2,1)}), bf16[2,512,4,256]{3,1,0,2:T(8,128)(2,1)}, u32[]{:S(2)}, u32[]{:S(2)}) %all-to-all-start.1) | async-done | bytes 2097184 | tf_op jit(solution)/shard_map/all_to_all | solution.py:103
  114.1 3.1 copy.50
  117.2 4.0 %reshape.123 = bf16[2,2048,2,128]{3,2,1,0:T(2,128)(2,1)} reshape(bf16[2,4,512,1,256]{4,2,1,0,3:T(8,128)(2,1)} %copy.50) | data formatting | bytes 4194304 | tf_op jit(solution)/shard_map/reshape | solution.py:106
  121.1 0.0 copy-done.2
  121.2 0.0 copy-start.4
  121.2 0.0 copy-start.1
  121.2 36.0 %while.10 = (s32[]{:T(128)}, bf16[2,64,2,16,128]{4,3,2,1,0:T(8,128)(2,1)}, s32[2]{0:T(128)S(1)}, bf16[2,2048,2,128]{3,2,1,0:T(2,128)(2,1)S(1)}, s32[2]{0:T(128)S...) while((s32[]{:T(128)}, ...), condition=%wide.region_8.9_spmd, body=%wide.region_3.8_spmd.sunk | while | flops 2266765312 | bytes 64308048 | solution.py:117
  121.2 2.5 constant_dynamic-slice_fusion.11
  123.7 0.6 dynamic_slice.52
  124.3 0.6 iota_compare_fusion.5
  125.0 2.9 bitcast_reduce_fusion.2
  127.9 0.1 constant_dynamic-slice_fusion.12
  127.9 0.6 dynamic_slice.53
  128.5 0.6 iota_compare_fusion.6
  129.2 0.1 fusion.46
  129.2 0.6 fusion.47
  129.9 0.2 fusion.49
  130.1 3.8 %fusion.48 = f32[2,16,64]{2,1,0:T(8,128)S(1)} fusion(f32[2,2048,64,16]{1,2,3,0:T(8,128)S(1)} %get-tuple-element.187, f32[2,16,64]{2,1,0:T(8,128)S(1)} %max.9, pred[2048]{0:T(1024)(128)(4,1)S(1)} %iota_compare_fusion.5), kind=kLoop, calls=%fused_computation.6.clone.1 | loop fusion | flops 16775168 | bytes 16795648 | tf_op jit(solution)/shard_map/while/body/eval_jaxpr/reduce_sum | solution.py:54
  133.9 3.7 %fusion.50 = f32[2,128,16,64]{1,3,2,0:T(8,128)S(1)} fusion(f32[2,2048,64,16]{1,2,3,0:T(8,128)S(1)} %get-tuple-element.187, f32[2,16,64]{2,1,0:T(8,128)S(1)} %add.142, f32[2,16,64]{2,1,0:T(8,128)S(1)} %max.9, pred[2048]{0:T(1024)(128)(4,1)S(1)} %iota_compare_fusion.5, bf16[1,2048,2,128]{3,2,1,0:T(2,128)(2,1)S(1)} %get-tuple-element.192), kind=kOutput, calls=%fused_computation.7.clone.1 | convolution fusion | flops 1094713344 | bytes 18892800 | tf_op jit(solution)/shard_map/while/body/eval_jaxpr/kgql,lkd->qkgd/dot_general | solution.py:59
  137.6 0.4 fusion.51
  138.0 1.2 copy_dynamic-update-slice_fusion.2
  139.2 2.5 constant_dynamic-slice_fusion.11
  141.7 0.6 dynamic_slice.52
  142.3 0.6 iota_compare_fusion.5
  143.0 2.9 bitcast_reduce_fusion.2
  145.9 0.1 constant_dynamic-slice_fusion.12
  145.9 0.6 dynamic_slice.53
  146.5 0.6 iota_compare_fusion.6
  147.1 0.1 fusion.46
  147.2 0.6 fusion.47
  147.9 0.2 fusion.49
  148.1 3.8 %fusion.48 = f32[2,16,64]{2,1,0:T(8,128)S(1)} fusion(f32[2,2048,64,16]{1,2,3,0:T(8,128)S(1)} %get-tuple-element.187, f32[2,16,64]{2,1,0:T(8,128)S(1)} %max.9, pred[2048]{0:T(1024)(128)(4,1)S(1)} %iota_compare_fusion.5), kind=kLoop, calls=%fused_computation.6.clone.1 | loop fusion | flops 16775168 | bytes 16795648 | tf_op jit(solution)/shard_map/while/body/eval_jaxpr/reduce_sum | solution.py:54
  151.9 3.7 %fusion.50 = f32[2,128,16,64]{1,3,2,0:T(8,128)S(1)} fusion(f32[2,2048,64,16]{1,2,3,0:T(8,128)S(1)} %get-tuple-element.187, f32[2,16,64]{2,1,0:T(8,128)S(1)} %add.142, f32[2,16,64]{2,1,0:T(8,128)S(1)} %max.9, pred[2048]{0:T(1024)(128)(4,1)S(1)} %iota_compare_fusion.5, bf16[1,2048,2,128]{3,2,1,0:T(2,128)(2,1)S(1)} %get-tuple-element.192), kind=kOutput, calls=%fused_computation.7.clone.1 | convolution fusion | flops 1094713344 | bytes 18892800 | tf_op jit(solution)/shard_map/while/body/eval_jaxpr/kgql,lkd->qkgd/dot_general | solution.py:59
  155.6 0.4 fusion.51
  156.0 1.2 copy_dynamic-update-slice_fusion.2
  157.2 2.4 reshape.127
  159.5 0.0 all-gather.2.cloned.1.call-update
  159.6 0.2 reduce-scatter.2.cloned.1.call-start
  159.8 0.0 copy-done
  159.8 0.0 copy-done.4
  159.8 0.0 copy-done.1
  159.8 0.1 fusion.37
  159.9 0.1 select_reduce_fusion.1
  160.1 55.9 %all-gather.2.cloned.1.call-done = bf16[1024,4096]{1,0:T(8,128)(2,1)} async-done(((bf16[128,4096]{1,0:T(8,128)(2,1)}), bf16[1024,4096]{1,0:T(8,128)(2,1)}) %all-gather.2.cloned.1.call-update) | async-done | bytes 8388624 | tf_op jit(solution)/shard_map/all_gather | solution.py:124
  216.0 16.5 %gather_fusion = bf16[768,4096]{1,0:T(8,128)(2,1)} fusion(bf16[1024,4096]{1,0:T(8,128)(2,1)} %all-gather.2.cloned.1.call-done, s32[1024]{0:T(1024)S(1)} %pad_clamp_fusion), kind=kCustom, calls=%fused_computation | custom fusion | bytes 12585984 | tf_op jit(solution)/shard_map/jit(_take)/gather | solution.py:127
  232.5 19.8 %fusion.20 = bf16[768,2048]{1,0:T(8,128)(2,1)} fusion(bf16[4096,2048]{1,0:T(8,128)(2,1)} %param.17, bf16[768,4096]{1,0:T(8,128)(2,1)} %gather_fusion, pred[768]{0:T(1024)(128)(4,1)S(1)} %compare_and_fusion.1, pred[768]{0:T(1024)(128)(4,1)S(1)} %get-tuple-element.109), kind=kOutput, calls=%fused_computation.43 | convolution fusion | flops 12892766208 | bytes 26215936 | tf_op jit(solution)/shard_map/dot_general | solution.py:130
  252.2 0.0 reduce-scatter.2.cloned.1.call-update
  252.3 59.9 %reduce-scatter.2.cloned.1.call-done = bf16[192,2048]{1,0:T(8,128)(2,1)} async-done(((bf16[768,2048]{1,0:T(8,128)(2,1)}), bf16[192,2048]{1,0:T(8,128)(2,1)}) %reduce-scatter.2.cloned.1.call-update) | async-done | bytes 786448 | tf_op jit(solution)/shard_map/reduce_scatter | solution.py:129
  (16 shorter events, 0.2 us)
Async XLA Ops:
  11.8 50.2 %all-to-all-start = ((bf16[2,512,4,256]{3,1,0,2:T(8,128)(2,1)}), bf16[2,512,4,256]{3,1,0,2:T(8,128)(2,1)S(1)}, u32[]{:S(2)}, u32[]{:S(2)}) async-start(bf16[2,512,4,256]{3,1,0,2:T(8,128)(2,1)} %copy.46), calls=%async_computation | async-start | bytes 4194304 | tf_op jit(solution)/shard_map/all_to_all | solution.py:104
  17.1 55.0 %copy-start.3 = (s32[16]{0:T(128)S(1)}, s32[16]{0:T(128)}, u32[]{:S(2)}) copy-start(s32[16]{0:T(128)} %param.19) | copy-start | bytes 196
  62.0 52.1 %all-to-all-start.1 = ((bf16[2,512,4,256]{3,1,0,2:T(8,128)(2,1)}), bf16[2,512,4,256]{3,1,0,2:T(8,128)(2,1)}, u32[]{:S(2)}, u32[]{:S(2)}) async-start(bf16[2,512,4,256]{3,1,0,2:T(8,128)(2,1)} %copy.49), calls=%async_computation.1 | async-start | bytes 4194304 | tf_op jit(solution)/shard_map/all_to_all | solution.py:103
  69.7 146.3 %all-gather.2.cloned.1.call-start = ((), (), s32[]{:S(2)}) async-start(), calls=%async_computation.3 | async-start | bytes 9437184 | tf_op jit(solution)/shard_map/all_gather | solution.py:124
  72.2 49.0 %copy-start.2 = (s32[2]{0:T(128)S(1)}, s32[2]{0:T(128)}, u32[]{:S(2)}) copy-start(s32[2]{0:T(128)} %param.18) | copy-start | bytes 28
  121.2 38.6 %copy-start = (s32[16]{0:T(128)S(1)}, s32[16]{0:T(128)}, u32[]{:S(2)}) copy-start(s32[16]{0:T(128)} %param.21) | copy-start | bytes 196
  121.2 38.6 %copy-start.4 = (s32[16]{0:T(128)S(1)}, s32[16]{0:T(128)}, u32[]{:S(2)}) copy-start(s32[16]{0:T(128)} %param.19) | copy-start | bytes 196
  121.2 38.7 %copy-start.1 = (s32[16]{0:T(128)S(1)}, s32[16]{0:T(128)}, u32[]{:S(2)}) copy-start(s32[16]{0:T(128)} %param.20) | copy-start | bytes 196
  159.6 152.6 %reduce-scatter.2.cloned.1.call-start = ((), (), s32[]{:S(2)}) async-start(), calls=%async_computation.4 | async-start | bytes 3932160 | tf_op jit(solution)/shard_map/reduce_scatter | solution.py:129
Sparse Core Ops, SparseCore 0:
  159.7 56.2 all-gather.1
  252.4 59.7 reduce-scatter.1
where the time goes:
time: 322 us; the launch traced here: 319 us
  waiting for transfers between devices  191 us (59%)
  local copies, waits for them, and re-layouts  55.6 us (17%)
  matrix products  34.9 us (11%)
  between operations  13.5 us (4%)
  starting transfers between devices  13.2 us (4%)
  other arithmetic  11 us (3%)
    reduce_scatter x1, waiting for transfers between devices, body(): lax.psum_scatter(jnp.dot(picked, out_weight, preferred_element_type=jnp.f...  59.9 us
    all_gather x1, waiting for transfers between devices, body(): home_all = lax.all_gather(attended_rows, 'dp', axis=0, tiled=True)  55.9 us
    all_to_all x1, waiting for transfers between devices, body(): lax.all_to_all(spread(cache_keys), 'tensor', split_axis=2, concat_axis=1,...  37.9 us
    all_to_all x1, waiting for transfers between devices, body(): lax.all_to_all(spread(cache_values), 'tensor', split_axis=2, concat_axis=...  36.8 us
    dot_general x1, matrix products, body(): jnp.dot(picked, out_weight, preferred_element_type=jnp.float32)  19.8 us
    gather x1, local copies, waits for them, and re-layouts, body(): picked = jnp.take(home_all, request * DRAFT + within, axis=0)  16.5 us
    unnamed x13, local copies, waits for them, and re-layouts  8.29 us
    all_to_all x1, starting transfers between devices, body(): lax.all_to_all(spread(cache_keys), 'tensor', split_axis=2, concat_axis=1,...  7.68 us
  transfers between devices with their start and end apart: 4, of which 4 were waited for; matrix products, arithmetic and copies ran while one was open for 5% of the time, Pallas kernels for 0%

commit v1 on v0

v1 whole, which is shorter than its diff:
```python
import functools
import math

import jax
import jax.numpy as jnp
from jax import lax
from jax.experimental import pallas as pl
from jax.experimental.pallas import tpu as pltpu
from jax.sharding import PartitionSpec as P

HEADS = 128
KV_HEADS = 8
HEAD_DIM = 128
DRAFT = 64
GROUP_REQ = 2
PACK = 96
NEG_FILL = -1e30
MESH = pl.DeviceIdType.MESH
AHEAD = 2


def kernel(
    dp_count,
    tensor_count,
    q_ref,
    dk_ref,
    dv_ref,
    ck_ref,
    cv_ref,
    w_ref,
    clen_ref,
    dlen_ref,
    dgroup_ref,
    doffset_ref,
    o_ref,
    kbuf,
    vbuf,
    wbuf,
    home,
    packed,
    acc,
    own,
    from_left,
    from_right,
    local_sem,
    w_sem,
    kv_send,
    kv_recv,
    ag_send,
    ag_recv,
    fw_send,
    fw_recv,
    rs_send,
    rs_recv,
):
    D, T = dp_count, tensor_count
    half = D // 2
    me = lax.axis_index("dp")
    rank = lax.axis_index("tensor")
    place, parity = me // 2, me % 2
    sibling = me + 1 - 2 * parity
    kv_local = kbuf.shape[0]
    span = ck_ref.shape[1]
    cache = kbuf.shape[2]
    width = packed.shape[2]
    per_kv = width // HEAD_DIM
    local_heads = per_kv * kv_local
    group_heads = HEADS // KV_HEADS
    block_rows = own.shape[1]
    out_cols = own.shape[2]
    tile = min(512, out_cols)
    tiles = out_cols // tile
    chunks = kv_local * GROUP_REQ
    kv_first = rank * local_heads // group_heads

    def peer(offset):
        return 2 * lax.rem(place + offset + half, half) + parity

    barrier = pltpu.get_barrier_semaphore()
    for o in range(1, T):
        pl.semaphore_signal(
            barrier, inc=1, device_id=(me, lax.rem(rank + o, T)), device_id_type=MESH
        )
    for o in range(1, half):
        pl.semaphore_signal(barrier, inc=1, device_id=(peer(o), rank), device_id_type=MESH)
    pl.semaphore_signal(barrier, inc=1, device_id=(sibling, rank), device_id_type=MESH)
    pl.semaphore_wait(barrier, T - 1 + half)

    sources = ((ck_ref, kbuf), (cv_ref, vbuf))

    def kv_copy(c, o, which):
        k, b = divmod(c, GROUP_REQ)
        target = lax.rem(rank + o, T)
        head = target * local_heads // group_heads + k
        src, dst = sources[which]
        return pltpu.make_async_remote_copy(
            src_ref=src.at[b, :, pl.ds(pl.multiple_of(head * HEAD_DIM, HEAD_DIM), HEAD_DIM)],
            dst_ref=dst.at[k, b, pl.ds(pl.multiple_of(rank * span, span), span), :],
            send_sem=kv_send.at[c, o, which],
            recv_sem=kv_recv.at[c, o, which],
            device_id=(me, target),
            device_id_type=MESH,
        )

    def kv_arrival(c, o, which):
        k, b = divmod(c, GROUP_REQ)
        origin = lax.rem(rank - o + T, T)
        dst = sources[which][1]
        landing = dst.at[k, b, pl.ds(pl.multiple_of(origin * span, span), span), :]
        return pltpu.make_async_remote_copy(
            src_ref=landing,
            dst_ref=landing,
            send_sem=kv_send.at[c, o, which],
            recv_sem=kv_recv.at[c, o, which],
            device_id=(me, origin),
            device_id_type=MESH,
        )

    def kv_local_copy(c, which):
        k, b = divmod(c, GROUP_REQ)
        src, dst = sources[which]
        return pltpu.make_async_copy(
            src.at[
                b, :, pl.ds(pl.multiple_of((kv_first + k) * HEAD_DIM, HEAD_DIM), HEAD_DIM)
            ],
            dst.at[k, b, pl.ds(pl.multiple_of(rank * span, span), span), :],
            local_sem.at[c, which],
        )

    def start_kv(c):
        for which in range(2):
            for o in range(T - 1, 0, -1):
                kv_copy(c, o, which).start()
            kv_local_copy(c, which).start()

    def wait_kv(c):
        for which in range(2):
            for o in range(1, T):
                kv_arrival(c, o, which).wait_recv()
            kv_local_copy(c, which).wait()

    def w_copy(k):
        return pltpu.make_async_copy(
            w_ref.at[pl.ds(k * width, width), :], wbuf.at[k], w_sem.at[k]
        )

    head_block = min(4, per_kv)
    rows = head_block * DRAFT
    rate = HEAD_DIM ** (-0.5) * math.log2(math.e)
    nt = (((1,), (1,)), ((), ()))

    def attend(c):
        k, b = divmod(c, GROUP_REQ)
        cache_len = clen_ref[b]
        draft_len = dlen_ref[me * GROUP_REQ + b]
        pos = lax.broadcasted_iota(jnp.int32, (1, cache), 1)
        bias = jnp.where(pos < cache_len, 0.0, NEG_FILL).astype(jnp.float32)
        slot = lax.rem(lax.broadcasted_iota(jnp.int32, (rows, DRAFT), 0), DRAFT)
        key_slot = lax.broadcasted_iota(jnp.int32, (rows, DRAFT), 1)
        keep = (key_slot <= slot) & (key_slot < draft_len)
        draft_bias = jnp.where(keep, 0.0, NEG_FILL).astype(jnp.float32)
        live_slot = lax.rem(lax.broadcasted_iota(jnp.int32, (rows, HEAD_DIM), 0), DRAFT)
        is_live = live_slot < draft_len
        draft_cols = pl.ds(pl.multiple_of((kv_first + k) * HEAD_DIM, HEAD_DIM), HEAD_DIM)
        draft_rows = pl.ds(b * DRAFT, DRAFT)

        def step(j, carry):
            blocks = []
            for h in range(head_block):
                col = pl.multiple_of((k * per_kv + j * head_block + h) * HEAD_DIM, HEAD_DIM)
                blocks.append(q_ref[draft_rows, pl.ds(col, HEAD_DIM)])
            q = jnp.concatenate(blocks, axis=0)
            s = lax.dot_general(q, kbuf[k, b], nt, preferred_element_type=jnp.float32) + bias
            sd = (
                lax.dot_general(
                    q, dk_ref[draft_rows, draft_cols], nt, preferred_element_type=jnp.float32
                )
                + draft_bias
            )
            m = jnp.maximum(
                jnp.max(s, axis=1, keepdims=True), jnp.max(sd, axis=1, keepdims=True)
            )
            p = jnp.exp2((s - m) * rate)
            pd = jnp.exp2((sd - m) * rate)
            total = jnp.sum(p, axis=1, keepdims=True) + jnp.sum(pd, axis=1, keepdims=True)
            mixed = jnp.dot(
                p.astype(jnp.bfloat16), vbuf[k, b], preferred_element_type=jnp.float32
            ) + jnp.dot(
                pd.astype(jnp.bfloat16),
                dv_ref[draft_rows, draft_cols],
                preferred_element_type=jnp.float32,
            )
            mixed = jnp.where(is_live, mixed / total, 0.0).astype(jnp.bfloat16)
            for h in range(head_block):
                col = pl.multiple_of((j * head_block + h) * HEAD_DIM, HEAD_DIM)
                home[c, me, :, pl.ds(col, HEAD_DIM)] = mixed[h * DRAFT : (h + 1) * DRAFT]
            return carry

        lax.fori_loop(0, per_kv // head_block, step, 0)

    def block_copy(c, origin, target, send, recv):
        return pltpu.make_async_remote_copy(
            src_ref=home.at[c, origin],
            dst_ref=home.at[c, origin],
            send_sem=send,
            recv_sem=recv,
            device_id=(target, rank),
            device_id_type=MESH,
        )

    def ag_copy(c, o):
        target = sibling if o == 0 else peer(o)
        return block_copy(c, me, target, ag_send.at[c, o], ag_recv.at[c, o])

    def ag_arrival(c, o):
        origin = sibling if o == 0 else peer(-o)
        return block_copy(c, origin, origin, ag_send.at[c, o], ag_recv.at[c, o])

    def fw_copy(c, o):
        return block_copy(c, peer(-o), sibling, fw_send.at[c, o], fw_recv.at[c, o])

    def fw_arrival(c, o):
        origin = peer(-o) + 1 - 2 * parity
        return block_copy(c, origin, sibling, fw_send.at[c, o], fw_recv.at[c, o])

    def start_ag(c):
        for o in range(half - 1, -1, -1):
            ag_copy(c, o).start()

    def finish_ag(c):
        for o in range(1, half):
            ag_arrival(c, o).wait_recv()
            fw_copy(c, o).start()
        ag_arrival(c, 0).wait_recv()
        for o in range(1, half):
            fw_arrival(c, o).wait_recv()

    source_rows = D * DRAFT

    def pack(c):
        b = c % GROUP_REQ
        column = lax.broadcasted_iota(jnp.int32, (1, source_rows), 1)
        group, slot = column // DRAFT, lax.rem(column, DRAFT)
        goal = jnp.full((1, source_rows), -1, jnp.int32)
        for g in range(D):
            r = g * GROUP_REQ + b
            first = dgroup_ref[r] * PACK + doffset_ref[r]
            goal = jnp.where((group == g) & (slot < dlen_ref[r]), slot + first, goal)

        def step(t, carry):
            row = lax.broadcasted_iota(jnp.int32, (block_rows, source_rows), 0)
            chosen = jnp.where(row + t * block_rows == goal, 1.0, 0.0).astype(jnp.bfloat16)
            got = jnp.dot(
                chosen,
                home[c].reshape(source_rows, width),
                preferred_element_type=jnp.float32,
            )
            if b == 0:
                packed[t] = got.astype(jnp.bfloat16)
            else:
                packed[t] = (packed[t].astype(jnp.float32) + got).astype(jnp.bfloat16)
            return carry

        lax.fori_loop(0, T, step, 0)

    def project(k):
        w_copy(k).wait()

        def step(i, carry):
            t, n = i // tiles, lax.rem(i, tiles)
            cols = pl.ds(pl.multiple_of(n * tile, tile), tile)
            part = jnp.dot(packed[t], wbuf[k, :, cols], preferred_element_type=jnp.float32)
            if k > 0:
                part = part + acc[t, :, cols]
            acc[t, :, cols] = part
            return carry

        lax.fori_loop(0, T * tiles, step, 0)

    def piece(n):
        return pl.ds(pl.multiple_of(n * tile, tile), tile)

    def rs_copy(direction, s, n):
        landing = from_left if direction == 0 else from_right
        target = rank + 1 if direction == 0 else rank - 1
        return pltpu.make_async_remote_copy(
            src_ref=own.at[s, :, piece(n)],
            dst_ref=landing.at[s, :, piece(n)],
            send_sem=rs_send.at[direction, s, n],
            recv_sem=rs_recv.at[direction, s, n],
            device_id=(me, target),
            device_id_type=MESH,
        )

    def rs_arrival(direction, s, n):
        landing = from_left if direction == 0 else from_right
        place_at = landing.at[s, :, piece(n)]
        origin = rank - 1 if direction == 0 else rank + 1
        return pltpu.make_async_remote_copy(
            src_ref=place_at,
            dst_ref=place_at,
            send_sem=rs_send.at[direction, s, n],
            recv_sem=rs_recv.at[direction, s, n],
            device_id=(me, origin),
            device_id_type=MESH,
        )

    def project_last(k):
        w_copy(k).wait()

        def step(i, carry):
            order, n = i // tiles, lax.rem(i, tiles)
            depth = order // 2
            s = jnp.where(lax.rem(order, 2) == 0, T - 1 - depth, depth)
            cols = piece(n)
            part = jnp.dot(packed[s], wbuf[k, :, cols], preferred_element_type=jnp.float32)
            if k > 0:
                part = part + acc[s, :, cols]
            own[s, :, cols] = part.astype(jnp.bfloat16)

            @pl.when((rank == 0) & (s > 0))
            def _():
                rs_copy(0, s, n).start()

            @pl.when((rank == T - 1) & (s < T - 1))
            def _():
                rs_copy(1, s, n).start()

            return carry

        lax.fori_loop(0, T * tiles, step, 0)

    def relay(i, carry):
        order, n = i // tiles, lax.rem(i, tiles)
        cols = piece(n)
        s_right, s_left = T - 1 - order, order

        @pl.when((rank > 0) & (s_right > rank))
        def _():
            rs_arrival(0, s_right, n).wait_recv()
            own[s_right, :, cols] = (
                own[s_right, :, cols].astype(jnp.float32)
                + from_left[s_right, :, cols].astype(jnp.float32)
            ).astype(jnp.bfloat16)
            rs_copy(0, s_right, n).start()

        @pl.when((rank < T - 1) & (s_left < rank))
        def _():
            rs_arrival(1, s_left, n).wait_recv()
            own[s_left, :, cols] = (
                own[s_left, :, cols].astype(jnp.float32)
                + from_right[s_left, :, cols].astype(jnp.float32)
            ).astype(jnp.bfloat16)
            rs_copy(1, s_left, n).start()

        return carry

    def settle(n, carry):
        cols = piece(n)
        acc[0, :, cols] = own[rank, :, cols].astype(jnp.float32)

        @pl.when(rank > 0)
        def _():
            rs_arrival(0, rank, n).wait_recv()
            acc[0, :, cols] = acc[0, :, cols] + from_left[rank, :, cols].astype(jnp.float32)

        @pl.when(rank < T - 1)
        def _():
            rs_arrival(1, rank, n).wait_recv()
            acc[0, :, cols] = acc[0, :, cols] + from_right[rank, :, cols].astype(jnp.float32)

        o_ref[:, cols] = acc[0, :, cols].astype(jnp.bfloat16)
        return carry

    def drain(i, carry):
        s, n = i // tiles, lax.rem(i, tiles)

        @pl.when(s > rank)
        def _():
            rs_copy(0, s, n).wait_send()

        @pl.when(s < rank)
        def _():
            rs_copy(1, s, n).wait_send()

        return carry

    for c in range(min(AHEAD, chunks)):
        start_kv(c)
    for k in range(kv_local):
        w_copy(k).start()

    def absorb(c):
        k, b = divmod(c, GROUP_REQ)
        finish_ag(c)
        pack(c)
        if b == GROUP_REQ - 1:
            if k == kv_local - 1:
                project_last(k)
            else:
                project(k)

    for c in range(chunks):
        wait_kv(c)
        if c + AHEAD < chunks:
            start_kv(c + AHEAD)
        attend(c)
        start_ag(c)
        if c > 0:
            absorb(c - 1)
    absorb(chunks - 1)
    lax.fori_loop(0, T * tiles, relay, 0)
    lax.fori_loop(0, tiles, settle, 0)
    lax.fori_loop(0, T * tiles, drain, 0)
    for c in range(chunks):
        for which in range(2):
            for o in range(1, T):
                kv_copy(c, o, which).wait_send()
        for o in range(half):
            ag_copy(c, o).wait_send()
        for o in range(1, half):
            fw_copy(c, o).wait_send()


def body(
    queries,
    draft_keys,
    draft_values,
    cache_keys,
    cache_values,
    out_weight,
    cache_lengths,
    draft_lengths,
    dest_group,
    dest_offset,
):
    T = lax.axis_size("tensor")
    D = lax.axis_size("dp")
    local_heads = HEADS // T
    group_heads = HEADS // KV_HEADS
    kv_local = max(1, local_heads // group_heads)
    width = local_heads // kv_local * HEAD_DIM
    cache = cache_keys.shape[1] * T
    out_cols = out_weight.shape[1]
    block_rows = PACK * D // T
    tiles = out_cols // min(512, out_cols)
    chunks = kv_local * GROUP_REQ
    half = D // 2
    vmem = pl.BlockSpec(memory_space=pltpu.VMEM)
    smem = pl.BlockSpec(memory_space=pltpu.SMEM)
    anywhere = pl.BlockSpec(memory_space=pl.ANY)
    dma = pltpu.SemaphoreType.DMA
    bf16 = jnp.bfloat16
    return pl.pallas_call(
        functools.partial(kernel, D, T),
        out_shape=jax.ShapeDtypeStruct((block_rows, out_cols), bf16),
        in_specs=[vmem] * 3 + [anywhere] * 3 + [smem] * 4,
        out_specs=vmem,
        scratch_shapes=[
            pltpu.VMEM((kv_local, GROUP_REQ, cache, HEAD_DIM), bf16),
            pltpu.VMEM((kv_local, GROUP_REQ, cache, HEAD_DIM), bf16),
            pltpu.VMEM((kv_local, width, out_cols), bf16),
            pltpu.VMEM((chunks, D, DRAFT, width), bf16),
            pltpu.VMEM((T, block_rows, width), bf16),
            pltpu.VMEM((T, block_rows, out_cols), jnp.float32),
            pltpu.VMEM((T, block_rows, out_cols), bf16),
            pltpu.VMEM((T, block_rows, out_cols), bf16),
            pltpu.VMEM((T, block_rows, out_cols), bf16),
            dma((chunks, 2)),
            dma((kv_local,)),
            dma((chunks, T, 2)),
            dma((chunks, T, 2)),
            dma((chunks, half)),
            dma((chunks, half)),
            dma((chunks, half)),
            dma((chunks, half)),
            dma((2, T, tiles)),
            dma((2, T, tiles)),
        ],
        compiler_params=pltpu.CompilerParams(
            collective_id=0, has_side_effects=True, vmem_limit_bytes=60 * 2**20
        ),
    )(
        queries,
        draft_keys,
        draft_values,
        cache_keys,
        cache_values,
        out_weight,
        cache_lengths,
        draft_lengths,
        dest_group,
        dest_offset,
    )


def solution(mesh):
    in_specs = (
        P("dp", "tensor"),
        P("dp", None),
        P("dp", None),
        P("dp", "tensor", None),
        P("dp", "tensor", None),
        P("tensor", "dp"),
        P("dp"),
        P(),
        P(),
        P(),
    )
    out_specs = P("tensor", "dp")
    return jax.shard_map(body, mesh=mesh, in_specs=in_specs, out_specs=out_specs, check_vma=False)
```

time: 322 us -> 192 us (0.60)
  waiting for transfers between devices: 191 us -> 0 us
  Pallas kernels: 0 us -> 190 us
  local copies, waits for them, and re-layouts: 55.6 us -> 2.09 us
  matrix products: 34.9 us -> 0 us
  between operations: 13.5 us -> 0.01 us
  starting transfers between devices: 13.2 us -> 0 us
  other arithmetic: 11 us -> 0 us
    pallas_call x0 -> x1, Pallas kernels: none -> 190 us  [body(): pl.pallas_call(functools.partial(kernel, D, T), out_shape=jax.ShapeDtypeS...]
    all_to_all x2 -> x0, waiting for transfers between devices: 74.7 us -> none  [the longest x1 37.9 us: body(): lax.all_to_all(spread(cache_keys), 'tensor', split_axis=2, concat_axis=1,...]
    reduce_scatter x1 -> x0, waiting for transfers between devices: 59.9 us -> none  [body(): lax.psum_scatter(jnp.dot(picked, out_weight, preferred_element_type=jnp.f...]
    all_gather x1 -> x0, waiting for transfers between devices: 55.9 us -> none  [body(): home_all = lax.all_gather(attended_rows, 'dp', axis=0, tiled=True)]
    dot_general x9 -> x0, matrix products: 34.9 us -> none  [the longest x1 19.8 us: body(): jnp.dot(picked, out_weight, preferred_element_type=jnp.float32)]
    gather x1 -> x0, local copies, waits for them, and re-layouts: 16.5 us -> none  [body(): picked = jnp.take(home_all, request * DRAFT + within, axis=0)]
    reshape x7 -> x0, local copies, waits for them, and re-layouts: 15.4 us -> none  [the longest x2 6.51 us: spread(): return cache_block.reshape(GROUP_REQ, span_rows, tensor_count, kv_width)]
    all_to_all x2 -> x0, starting transfers between devices: 13 us -> none  [the longest x1 7.68 us: body(): lax.all_to_all(spread(cache_keys), 'tensor', split_axis=2, concat_axis=1,...]
  transfers between devices with their start and end apart: 4 -> 0, of which waited for: 4 -> 0; matrix products, arithmetic and copies ran while one was open for 5% -> 0% of each run, Pallas kernels for 0% -> 0%
where the time goes in v1:
time: 192 us
  Pallas kernels  190 us (99%)
  local copies, waits for them, and re-layouts  2.09 us (1%)
    pallas_call x1, Pallas kernels, body(): pl.pallas_call(functools.partial(kernel, D, T), out_shape=jax.ShapeDtypeS...  190 us

profile of v1, /device:TPU:10, one launch (start us, length us, event | category | flops | bytes accessed | tf_op | source)
XLA Modules:
  0.0 192.2 jit_solution(13252157627482200662)
XLA Ops:
  0.0 190.1 %shard_map.100 = bf16[192,2048]{1,0:T(8,128)(2,1)} custom-call(bf16[128,4096]{1,0:T(8,128)(2,1)} %q_ref.1, bf16[128,1024]{1,0:T(8,128)(2,1)} %dk_ref.1, bf16[128,1024]{1,0:T(8,128)(2,1)} %dv_ref.1, bf16[2,512,1024]{2,1,0:T(8,128)(2,1)} %ck_ref.1, bf16[2,512,1024]{2,1,0:T(8,128)(2,1)} %cv_ref.1, bf16[4096,2048]{1,0:T(8,128)(2,1)} %w_ref.1, s32[2]{0:T(128)} %clen_ref.1, ...), custom_call_target="tpu_custom_call" | custom-call | tf_op jit(solution)/shard_map/pallas_call | solution.py:454
  190.1 2.1 %copy.12 = bf16[192,2048]{1,0:T(8,128)(2,1)} copy(bf16[192,2048]{1,0:T(8,128)(2,1)} %shard_map.100) | data formatting | bytes 1572864

commit v2 on v1

--- a/solution.py
+++ b/solution.py
@@ -16,7 +16,7 @@
 PACK = 96
 NEG_FILL = -1e30
 MESH = pl.DeviceIdType.MESH
-AHEAD = 2
+SLAB = 768
 
 
 def kernel(
@@ -37,6 +37,9 @@
     vbuf,
     wbuf,
     home,
+    weights,
+    totals,
+    draft_part,
     packed,
     acc,
     own,
@@ -62,12 +65,14 @@
     kv_local = kbuf.shape[0]
     span = ck_ref.shape[1]
     cache = kbuf.shape[2]
-    width = packed.shape[2]
+    width = packed.shape[1]
     per_kv = width // HEAD_DIM
     local_heads = per_kv * kv_local
     group_heads = HEADS // KV_HEADS
-    block_rows = own.shape[1]
-    out_cols = own.shape[2]
+    all_rows, out_cols = own.shape
+    block_rows = all_rows // T
+    slab = min(SLAB, all_rows)
+    slabs = all_rows // slab
     tile = min(512, out_cols)
     tiles = out_cols // tile
     chunks = kv_local * GROUP_REQ
@@ -127,17 +132,15 @@
             local_sem.at[c, which],
         )
 
-    def start_kv(c):
-        for which in range(2):
-            for o in range(T - 1, 0, -1):
-                kv_copy(c, o, which).start()
-            kv_local_copy(c, which).start()
-
-    def wait_kv(c):
-        for which in range(2):
-            for o in range(1, T):
-                kv_arrival(c, o, which).wait_recv()
-            kv_local_copy(c, which).wait()
+    def start_kv(c, which):
+        for o in range(T - 1, 0, -1):
+            kv_copy(c, o, which).start()
+        kv_local_copy(c, which).start()
+
+    def wait_kv(c, which):
+        for o in range(1, T):
+            kv_arrival(c, o, which).wait_recv()
+        kv_local_copy(c, which).wait()
 
     def w_copy(k):
         return pltpu.make_async_copy(
@@ -149,7 +152,7 @@
     rate = HEAD_DIM ** (-0.5) * math.log2(math.e)
     nt = (((1,), (1,)), ((), ()))
 
-    def attend(c):
+    def score(c):
         k, b = divmod(c, GROUP_REQ)
         cache_len = clen_ref[b]
         draft_len = dlen_ref[me * GROUP_REQ + b]
@@ -159,8 +162,6 @@
         key_slot = lax.broadcasted_iota(jnp.int32, (rows, DRAFT), 1)
         keep = (key_slot <= slot) & (key_slot < draft_len)
         draft_bias = jnp.where(keep, 0.0, NEG_FILL).astype(jnp.float32)
-        live_slot = lax.rem(lax.broadcasted_iota(jnp.int32, (rows, HEAD_DIM), 0), DRAFT)
-        is_live = live_slot < draft_len
         draft_cols = pl.ds(pl.multiple_of((kv_first + k) * HEAD_DIM, HEAD_DIM), HEAD_DIM)
         draft_rows = pl.ds(b * DRAFT, DRAFT)
 
@@ -182,15 +183,32 @@
             )
             p = jnp.exp2((s - m) * rate)
             pd = jnp.exp2((sd - m) * rate)
+            at = pl.ds(pl.multiple_of(j * rows, rows), rows)
             total = jnp.sum(p, axis=1, keepdims=True) + jnp.sum(pd, axis=1, keepdims=True)
-            mixed = jnp.dot(
-                p.astype(jnp.bfloat16), vbuf[k, b], preferred_element_type=jnp.float32
-            ) + jnp.dot(
+            totals[at, :] = jnp.broadcast_to(total, (rows, HEAD_DIM))
+            weights[at, :] = p.astype(jnp.bfloat16)
+            draft_part[at, :] = jnp.dot(
                 pd.astype(jnp.bfloat16),
                 dv_ref[draft_rows, draft_cols],
                 preferred_element_type=jnp.float32,
             )
-            mixed = jnp.where(is_live, mixed / total, 0.0).astype(jnp.bfloat16)
+            return carry
+
+        lax.fori_loop(0, per_kv // head_block, step, 0)
+
+    def mix(c):
+        k, b = divmod(c, GROUP_REQ)
+        draft_len = dlen_ref[me * GROUP_REQ + b]
+        live_slot = lax.rem(lax.broadcasted_iota(jnp.int32, (rows, HEAD_DIM), 0), DRAFT)
+        is_live = live_slot < draft_len
+
+        def step(j, carry):
+            at = pl.ds(pl.multiple_of(j * rows, rows), rows)
+            mixed = (
+                jnp.dot(weights[at, :], vbuf[k, b], preferred_element_type=jnp.float32)
+                + draft_part[at, :]
+            )
+            mixed = jnp.where(is_live, mixed / totals[at, :], 0.0).astype(jnp.bfloat16)
             for h in range(head_block):
                 col = pl.multiple_of((j * head_block + h) * HEAD_DIM, HEAD_DIM)
                 home[c, me, :, pl.ds(col, HEAD_DIM)] = mixed[h * DRAFT : (h + 1) * DRAFT]
@@ -247,35 +265,46 @@
             first = dgroup_ref[r] * PACK + doffset_ref[r]
             goal = jnp.where((group == g) & (slot < dlen_ref[r]), slot + first, goal)
 
-        def step(t, carry):
-            row = lax.broadcasted_iota(jnp.int32, (block_rows, source_rows), 0)
-            chosen = jnp.where(row + t * block_rows == goal, 1.0, 0.0).astype(jnp.bfloat16)
-            got = jnp.dot(
-                chosen,
-                home[c].reshape(source_rows, width),
-                preferred_element_type=jnp.float32,
-            )
-            if b == 0:
-                packed[t] = got.astype(jnp.bfloat16)
-            else:
-                packed[t] = (packed[t].astype(jnp.float32) + got).astype(jnp.bfloat16)
-            return carry
-
-        lax.fori_loop(0, T, step, 0)
+        pack_tile = min(512, width)
+
+        def slab_step(t, carry):
+            at = pl.ds(pl.multiple_of(t * slab, slab), slab)
+            row = lax.broadcasted_iota(jnp.int32, (slab, source_rows), 0)
+            chosen = jnp.where(row + t * slab == goal, 1.0, 0.0).astype(jnp.bfloat16)
+
+            def step(n, carry):
+                cols = pl.ds(pl.multiple_of(n * pack_tile, pack_tile), pack_tile)
+                got = jnp.dot(
+                    chosen,
+                    home[c, :, :, cols].reshape(source_rows, pack_tile),
+                    preferred_element_type=jnp.float32,
+                )
+                if b > 0:
+                    got = got + packed[at, cols].astype(jnp.float32)
+                packed[at, cols] = got.astype(jnp.bfloat16)
+                return carry
+
+            return lax.fori_loop(0, width // pack_tile, step, carry)
+
+        lax.fori_loop(0, slabs, slab_step, 0)
 
     def project(k):
         w_copy(k).wait()
 
         def step(i, carry):
-            t, n = i // tiles, lax.rem(i, tiles)
+            n, t = i // slabs, lax.rem(i, slabs)
             cols = pl.ds(pl.multiple_of(n * tile, tile), tile)
-            part = jnp.dot(packed[t], wbuf[k, :, cols], preferred_element_type=jnp.float32)
+            at = pl.ds(pl.multiple_of(t * slab, slab), slab)
+            part = jnp.dot(packed[at, :], wbuf[k, :, cols], preferred_element_type=jnp.float32)
             if k > 0:
-                part = part + acc[t, :, cols]
-            acc[t, :, cols] = part
+                part = part + acc[at, cols]
+            acc[at, cols] = part
             return carry
 
-        lax.fori_loop(0, T * tiles, step, 0)
+        lax.fori_loop(0, slabs * tiles, step, 0)
+
+    def block(s):
+        return pl.ds(pl.multiple_of(s * block_rows, block_rows), block_rows)
 
     def piece(n):
         return pl.ds(pl.multiple_of(n * tile, tile), tile)
@@ -284,8 +313,8 @@
         landing = from_left if direction == 0 else from_right
         target = rank + 1 if direction == 0 else rank - 1
         return pltpu.make_async_remote_copy(
-            src_ref=own.at[s, :, piece(n)],
-            dst_ref=landing.at[s, :, piece(n)],
+            src_ref=own.at[block(s), piece(n)],
+            dst_ref=landing.at[block(s), piece(n)],
             send_sem=rs_send.at[direction, s, n],
             recv_sem=rs_recv.at[direction, s, n],
             device_id=(me, target),
@@ -294,7 +323,7 @@
 
     def rs_arrival(direction, s, n):
         landing = from_left if direction == 0 else from_right
-        place_at = landing.at[s, :, piece(n)]
+        place_at = landing.at[block(s), piece(n)]
         origin = rank - 1 if direction == 0 else rank + 1
         return pltpu.make_async_remote_copy(
             src_ref=place_at,
@@ -308,48 +337,51 @@
     def project_last(k):
         w_copy(k).wait()
 
-        def step(i, carry):
-            order, n = i // tiles, lax.rem(i, tiles)
-            depth = order // 2
-            s = jnp.where(lax.rem(order, 2) == 0, T - 1 - depth, depth)
+        def step(n, carry):
             cols = piece(n)
-            part = jnp.dot(packed[s], wbuf[k, :, cols], preferred_element_type=jnp.float32)
-            if k > 0:
-                part = part + acc[s, :, cols]
-            own[s, :, cols] = part.astype(jnp.bfloat16)
-
-            @pl.when((rank == 0) & (s > 0))
+            for t in range(slabs):
+                at = pl.ds(t * slab, slab)
+                part = jnp.dot(
+                    packed[at, :], wbuf[k, :, cols], preferred_element_type=jnp.float32
+                )
+                if k > 0:
+                    part = part + acc[at, cols]
+                own[at, cols] = part.astype(jnp.bfloat16)
+
+            @pl.when(rank == 0)
             def _():
-                rs_copy(0, s, n).start()
-
-            @pl.when((rank == T - 1) & (s < T - 1))
+                for s in range(T - 1, 0, -1):
+                    rs_copy(0, s, n).start()
+
+            @pl.when(rank == T - 1)
             def _():
-                rs_copy(1, s, n).start()
+                for s in range(T - 1):
+                    rs_copy(1, s, n).start()
 
             return carry
 
-        lax.fori_loop(0, T * tiles, step, 0)
+        lax.fori_loop(0, tiles, step, 0)
 
     def relay(i, carry):
-        order, n = i // tiles, lax.rem(i, tiles)
+        n, order = i // T, lax.rem(i, T)
         cols = piece(n)
         s_right, s_left = T - 1 - order, order
 
         @pl.when((rank > 0) & (s_right > rank))
         def _():
             rs_arrival(0, s_right, n).wait_recv()
-            own[s_right, :, cols] = (
-                own[s_right, :, cols].astype(jnp.float32)
-                + from_left[s_right, :, cols].astype(jnp.float32)
+            own[block(s_right), cols] = (
+                own[block(s_right), cols].astype(jnp.float32)
+                + from_left[block(s_right), cols].astype(jnp.float32)
             ).astype(jnp.bfloat16)
             rs_copy(0, s_right, n).start()
 
         @pl.when((rank < T - 1) & (s_left < rank))
         def _():
             rs_arrival(1, s_left, n).wait_recv()
-            own[s_left, :, cols] = (
-                own[s_left, :, cols].astype(jnp.float32)
-                + from_right[s_left, :, cols].astype(jnp.float32)
+            own[block(s_left), cols] = (
+                own[block(s_left), cols].astype(jnp.float32)
+                + from_right[block(s_left), cols].astype(jnp.float32)
             ).astype(jnp.bfloat16)
             rs_copy(1, s_left, n).start()
 
@@ -357,19 +389,19 @@
 
     def settle(n, carry):
         cols = piece(n)
-        acc[0, :, cols] = own[rank, :, cols].astype(jnp.float32)
+        acc[:block_rows, cols] = own[block(rank), cols].astype(jnp.float32)
 
         @pl.when(rank > 0)
         def _():
             rs_arrival(0, rank, n).wait_recv()
-            acc[0, :, cols] = acc[0, :, cols] + from_left[rank, :, cols].astype(jnp.float32)
+            acc[:block_rows, cols] = acc[:block_rows, cols] + from_left[block(rank), cols].astype(jnp.float32)
 
         @pl.when(rank < T - 1)
         def _():
             rs_arrival(1, rank, n).wait_recv()
-            acc[0, :, cols] = acc[0, :, cols] + from_right[rank, :, cols].astype(jnp.float32)
-
-        o_ref[:, cols] = acc[0, :, cols].astype(jnp.bfloat16)
+            acc[:block_rows, cols] = acc[:block_rows, cols] + from_right[block(rank), cols].astype(jnp.float32)
+
+        o_ref[:, cols] = acc[:block_rows, cols].astype(jnp.bfloat16)
         return carry
 
     def drain(i, carry):
@@ -385,8 +417,8 @@
 
         return carry
 
-    for c in range(min(AHEAD, chunks)):
-        start_kv(c)
+    for which in range(2):
+        start_kv(0, which)
     for k in range(kv_local):
         w_copy(k).start()
 
@@ -401,13 +433,17 @@
                 project(k)
 
     for c in range(chunks):
-        wait_kv(c)
-        if c + AHEAD < chunks:
-            start_kv(c + AHEAD)
-        attend(c)
-        start_ag(c)
+        wait_kv(c, 0)
+        if c + 1 < chunks:
+            start_kv(c + 1, 0)
+        score(c)
         if c > 0:
             absorb(c - 1)
+        wait_kv(c, 1)
+        if c + 1 < chunks:
+            start_kv(c + 1, 1)
+        mix(c)
+        start_ag(c)
     absorb(chunks - 1)
     lax.fori_loop(0, T * tiles, relay, 0)
     lax.fori_loop(0, tiles, settle, 0)
@@ -461,11 +497,14 @@
             pltpu.VMEM((kv_local, GROUP_REQ, cache, HEAD_DIM), bf16),
             pltpu.VMEM((kv_local, width, out_cols), bf16),
             pltpu.VMEM((chunks, D, DRAFT, width), bf16),
-            pltpu.VMEM((T, block_rows, width), bf16),
-            pltpu.VMEM((T, block_rows, out_cols), jnp.float32),
-            pltpu.VMEM((T, block_rows, out_cols), bf16),
-            pltpu.VMEM((T, block_rows, out_cols), bf16),
-            pltpu.VMEM((T, block_rows, out_cols), bf16),
+            pltpu.VMEM((width // HEAD_DIM * DRAFT, cache), bf16),
+            pltpu.VMEM((width // HEAD_DIM * DRAFT, HEAD_DIM), jnp.float32),
+            pltpu.VMEM((width // HEAD_DIM * DRAFT, HEAD_DIM), jnp.float32),
+            pltpu.VMEM((T * block_rows, width), bf16),
+            pltpu.VMEM((T * block_rows, out_cols), jnp.float32),
+            pltpu.VMEM((T * block_rows, out_cols), bf16),
+            pltpu.VMEM((T * block_rows, out_cols), bf16),
+            pltpu.VMEM((T * block_rows, out_cols), bf16),
             dma((chunks, 2)),
             dma((kv_local,)),
             dma((chunks, T, 2)),

time: 192 us -> 201 us (1.047)
  the two profiles are of different devices: /device:TPU:10 before, /device:TPU:0 now
where the time goes in v2:
time: 201 us
  Pallas kernels  199 us (99%)
  local copies, waits for them, and re-layouts  2.09 us (1%)
    pallas_call x1, Pallas kernels, body(): pl.pallas_call(functools.partial(kernel, D, T), out_shape=jax.ShapeDtypeS...  199 us

profile of v2, /device:TPU:0, one launch (start us, length us, event | category | flops | bytes accessed | tf_op | source)
XLA Modules:
  0.0 200.8 jit_solution(13807243284122154716)
XLA Ops:
  0.0 198.7 %shard_map.100 = bf16[192,2048]{1,0:T(8,128)(2,1)} custom-call(bf16[128,4096]{1,0:T(8,128)(2,1)} %q_ref.1, bf16[128,1024]{1,0:T(8,128)(2,1)} %dk_ref.1, bf16[128,1024]{1,0:T(8,128)(2,1)} %dv_ref.1, bf16[2,512,1024]{2,1,0:T(8,128)(2,1)} %ck_ref.1, bf16[2,512,1024]{2,1,0:T(8,128)(2,1)} %cv_ref.1, bf16[4096,2048]{1,0:T(8,128)(2,1)} %w_ref.1, s32[2]{0:T(128)} %clen_ref.1, ...), custom_call_target="tpu_custom_call" | custom-call | tf_op jit(solution)/shard_map/pallas_call | solution.py:490
  198.7 2.1 %copy.12 = bf16[192,2048]{1,0:T(8,128)(2,1)} copy(bf16[192,2048]{1,0:T(8,128)(2,1)} %shard_map.100) | data formatting | bytes 1572864

commit v3 on v1

--- a/solution.py
+++ b/solution.py
@@ -16,7 +16,7 @@
 PACK = 96
 NEG_FILL = -1e30
 MESH = pl.DeviceIdType.MESH
-AHEAD = 2
+AHEAD = 1
 
 
 def kernel(

time: 192 us -> 188 us (0.979)
  Pallas kernels: 190 us -> 185 us
    pallas_call x1, Pallas kernels: 190 us -> 185 us  [body(): pl.pallas_call(functools.partial(kernel, D, T), out_shape=jax.ShapeDtypeS...]
where the time goes in v3:
time: 188 us
  Pallas kernels  185 us (98%)
  local copies, waits for them, and re-layouts  2.09 us (1%)
    pallas_call x1, Pallas kernels, body(): pl.pallas_call(functools.partial(kernel, D, T), out_shape=jax.ShapeDtypeS...  185 us

profile of v3, /device:TPU:10, one launch (start us, length us, event | category | flops | bytes accessed | tf_op | source)
XLA Modules:
  0.0 187.5 jit_solution(12873288176284886240)
XLA Ops:
  0.0 185.4 %shard_map.100 = bf16[192,2048]{1,0:T(8,128)(2,1)} custom-call(bf16[128,4096]{1,0:T(8,128)(2,1)} %q_ref.1, bf16[128,1024]{1,0:T(8,128)(2,1)} %dk_ref.1, bf16[128,1024]{1,0:T(8,128)(2,1)} %dv_ref.1, bf16[2,512,1024]{2,1,0:T(8,128)(2,1)} %ck_ref.1, bf16[2,512,1024]{2,1,0:T(8,128)(2,1)} %cv_ref.1, bf16[4096,2048]{1,0:T(8,128)(2,1)} %w_ref.1, s32[2]{0:T(128)} %clen_ref.1, ...), custom_call_target="tpu_custom_call" | custom-call | tf_op jit(solution)/shard_map/pallas_call | solution.py:454
  185.4 2.1 %copy.12 = bf16[192,2048]{1,0:T(8,128)(2,1)} copy(bf16[192,2048]{1,0:T(8,128)(2,1)} %shard_map.100) | data formatting | bytes 1572864
